TPU v7x, 32 devices: a whole 2x2x4 slice. The times are simulated.
32 devices in a mesh: az: 8 (over z, y), rad: 4 (over x, core).
Axes of the slice: x: 2, y: 2, z: 4, core: 2. Of those that a mesh axis runs over, the one named last changes fastest.
Arguments:
- combustor_state: float32 [9, 16, 32, 1024], P(None, None, 'rad', 'az'), may hold values from -6 to 6
- swirl_speed: float32 [16, 32, 1024], P(None, 'rad', 'az'), may hold values from -0.6 to 1
- reaction_rate: float32 [16, 32, 1024], P(None, 'rad', 'az'), may hold values from 0.1 to 1
- kinetics: float32 [9, 9], replicated, may hold values from -2 to 2
- stator_state: float32 [9, 16, 32, 2048], P(None, None, 'rad', 'az'), may hold values from -6 to 6
- inlet_index: int32 [8, 256], P('az'), may hold values from 0 to 254, as said below
- inlet_weight: float32 [8, 256], P('az'), may hold values from 0 to 1
Outputs:
- combustor_next: float32 [9, 16, 32, 1024], P(None, None, 'rad', 'az')
- stator_next: float32 [9, 16, 32, 2048], P(None, None, 'rad', 'az')
Inputs may be any that keep to these rules, and one draw needn't show every extreme that they name: Along j, inlet_index[p, j] never falls and rises by at most one from one pitch cell to the next.
All inputs are finite; a program needn't handle non-finite values.
Results may differ from a plain program's by a relative error of at most 0.0003.
Values sent between devices are 32-bit elements; how exact they have to be, the bound alone decides.
A program may use at most 64 MiB of HBM per device.

v0:
```python
import jax
import jax.numpy as jnp
from jax import lax
from jax.sharding import PartitionSpec as P

comb_step = 0.4
axial_speed = 0.5
radial_mix = 0.25
stator_speed = 0.5
pitch_mix = 0.2
stator_mix = 0.2


def extended_2(array, sides, width, wrap):
    for axis, dim in sides:
        size, length = (lax.axis_size(axis), array.shape[dim])
        up = [(i, (i + 1) % size) for i in range(size if wrap else size - 1)]
        down = [(j, i) for i, j in up]
        last = lax.slice_in_dim(array, length - width, length, axis=dim)
        first = lax.slice_in_dim(array, 0, width, axis=dim)
        before = lax.ppermute(last, axis, up)
        after = lax.ppermute(first, axis, down)
        array = jnp.concatenate([before, array, after], axis=dim)
    return array


def tendency(q_cycle, u_cycle, q_wall, reaction, kinetics):
    fplus = jnp.maximum(u_cycle, 0.0)[None] * q_cycle
    fminus = jnp.minimum(u_cycle, 0.0)[None] * q_cycle
    face_flux = (-fplus[..., 0:-3] + 5.0 * fplus[..., 1:-2] + 2.0 * fplus[..., 2:-1]) / 6.0 + (
        2.0 * fminus[..., 1:-2] + 5.0 * fminus[..., 2:-1] - fminus[..., 3:]
    ) / 6.0
    azimuthal = face_flux[..., :-1] - face_flux[..., 1:]
    centre = q_cycle[..., 2:-2]
    before = jnp.concatenate([jnp.zeros_like(centre[:, :1]), centre[:, :-1]], axis=1)
    axial_term = axial_speed * (before - centre)
    radial = radial_mix * (q_wall[:, :, 2:] - 2.0 * centre + q_wall[:, :, :-2])
    source = reaction[None] * jnp.einsum(
        "st,txyz->sxyz", kinetics, centre, precision=lax.Precision.HIGHEST
    )
    return azimuthal + axial_term + radial + source


def radial_rim(field):
    return extended_2(field, (("rad", 2),), 1, False)


def stator_update(current, below_edge, above_edge, inflow, walled):
    pitched = jnp.concatenate([below_edge, current, above_edge], axis=-1)
    before = jnp.concatenate([inflow[:, None], current[:, :-1]], axis=1)
    axial_term = stator_speed * (before - current)
    pitch_term = pitch_mix * (pitched[..., 2:] - 2.0 * current + pitched[..., :-2])
    radial = stator_mix * (walled[:, :, 2:] - 2.0 * current + walled[:, :, :-2])
    return current + (axial_term + pitch_term + radial)


def body(
    combustor_state, swirl_speed, reaction_rate, kinetics, stator_state, inlet_index, inlet_weight
):
    species = combustor_state.shape[0]
    tile_cells = combustor_state.shape[3]

    def section_rate(current):
        stacked = jnp.concatenate([current, swirl_speed[None]], axis=0)
        extended = extended_2(stacked, (("az", 3),), 2, True)
        return tendency(
            extended[:species], extended[species], radial_rim(current), reaction_rate, kinetics
        )

    section_one = combustor_state + comb_step * section_rate(combustor_state)
    combustor_next = 0.5 * combustor_state + 0.5 * (
        section_one + comb_step * section_rate(section_one)
    )
    exit_plane = combustor_next[:, -1]
    rim_cells = tile_cells // 2
    offsets = inlet_index[0]
    weights = inlet_weight[0]
    exit_rim = extended_2(exit_plane, (("az", 2),), rim_cells, True)
    left_value = jnp.take(exit_rim, offsets, axis=2)
    right_value = jnp.take(exit_rim, offsets + 1, axis=2)
    inflow = (1.0 - weights) * left_value + weights * right_value
    pitched = extended_2(stator_state, (("az", 3),), 1, True)
    below_edge = pitched[..., :1]
    above_edge = pitched[..., -1:]
    walled = extended_2(stator_state, (("rad", 2),), 1, False)
    stator_next = stator_update(stator_state, below_edge, above_edge, inflow, walled)
    return (combustor_next, stator_next)


def solution(mesh):
    in_specs = (
        P(None, None, "rad", "az"),
        P(None, "rad", "az"),
        P(None, "rad", "az"),
        P(),
        P(None, None, "rad", "az"),
        P("az", None),
        P("az", None),
    )
    out_specs = (P(None, None, "rad", "az"), P(None, None, "rad", "az"))
    return jax.shard_map(body, mesh=mesh, in_specs=in_specs, out_specs=out_specs, check_vma=False)
```

profile of v0, /device:TPU:0, one launch (start us, length us, event | category | flops | bytes accessed | tf_op | source)
XLA Modules:
  0.0 100.2 jit_solution(9249805482507403369)
XLA Ops:
  0.6 1.4 %copy.55 = f32[9,16,8,128]{3,0,2,1:T(8,128)S(1)} copy(f32[9,16,8,128]{3,2,1,0:T(8,128)} %param.9) | data formatting | bytes 1179648 | tf_op args[0]
  2.1 2.5 %slice_maximum_fusion.1 = (f32[10,16,8,2]{3,0,2,1:T(8,128)}, f32[10,16,8,2]{3,0,2,1:T(8,128)S(1)}) fusion(f32[9,16,8,128]{3,0,2,1:T(8,128)S(1)} %copy.55, f32[1,16,8,128]{3,0,2,1:T(1,128)} %bitcast.40), kind=kLoop, calls=%fused_computation.79 | loop fusion | flops 5120 | bytes 675840 | tf_op jit(solution)/shard_map/concatenate | solution.py:64
  4.6 2.5 %copy.38 = f32[10,16,8,2]{1,2,3,0:T(8,128)} copy(f32[10,16,8,2]{3,0,2,1:T(8,128)} %get-tuple-element.23) | data formatting | bytes 20480 | tf_op jit(solution)/shard_map/slice | solution.py:19
  7.1 3.0 %collective-permute-start = (f32[10,16,8,2]{1,2,3,0:T(8,128)}, f32[10,16,8,2]{1,2,3,0:T(8,128)}, u32[]{:S(2)}, u32[]{:S(2)}) collective-permute-start(f32[10,16,8,2]{1,2,3,0:T(8,128)} %copy.38), channel_id=1, source_target_pairs={{0,4},{4,8},{8,12},{12,16},{16,20},{20,24},{24,28},{28,0},{1,5},{5... | collective-permute-start | bytes 30728 | tf_op jit(solution)/shard_map/ppermute | solution.py:21
  10.1 1.3 %copy.39 = f32[10,16,8,2]{1,2,3,0:T(8,128)} copy(f32[10,16,8,2]{3,0,2,1:T(8,128)S(1)} %get-tuple-element.24) | data formatting | bytes 20480 | tf_op jit(solution)/shard_map/slice | solution.py:20
  11.4 3.0 %collective-permute-start.1 = (f32[10,16,8,2]{1,2,3,0:T(8,128)}, f32[10,16,8,2]{1,2,3,0:T(8,128)}, u32[]{:S(2)}, u32[]{:S(2)}) collective-permute-start(f32[10,16,8,2]{1,2,3,0:T(8,128)} %copy.39), channel_id=1, source_target_pairs={{4,0},{8,4},{12,8},{16,12},{20,16},{24,20},{28,24},{0,28},{5,1},{9... | collective-permute-start | bytes 30728 | tf_op jit(solution)/shard_map/ppermute | solution.py:22
  16.5 3.7 %collective-permute-start.3 = (f32[9,16,1,128]{3,0,2,1:T(8,128)}, f32[9,16,1,128]{3,0,2,1:T(8,128)}, u32[]{:S(2)}, u32[]{:S(2)}) collective-permute-start(f32[9,16,1,128]{3,0,2,1:T(8,128)} %get-tuple-element.28), channel_id=1, source_target_pairs={{0,1},{1,2},{2,3},{4,5},{5,6},{6,7},{8,9},{9,10},{10,11},{12,13},{... | collective-permute-start | bytes 221192 | tf_op jit(solution)/shard_map/ppermute | solution.py:21
  21.5 2.0 %collective-permute-start.10 = (f32[9,16,8,1]{1,2,3,0:T(8,128)}, f32[9,16,8,1]{1,2,3,0:T(8,128)S(1)}, u32[]{:S(2)}, u32[]{:S(2)}) collective-permute-start(f32[9,16,8,1]{1,2,3,0:T(8,128)} %copy.73), channel_id=1, source_target_pairs={{4,0},{8,4},{12,8},{16,12},{20,16},{24,20},{28,24},{0,28},{5,1},{9... | collective-permute-start | bytes 13832 | tf_op jit(solution)/shard_map/ppermute | solution.py:22
  26.1 1.9 %copy.40 = f32[10,16,8,2]{3,0,2,1:T(8,128)S(1)} copy(f32[10,16,8,2]{1,2,3,0:T(8,128)} %collective-permute-done) | data formatting | bytes 20480 | tf_op jit(solution)/shard_map/ppermute | solution.py:21
  29.4 2.8 %copy.41 = f32[10,16,8,2]{3,0,2,1:T(8,128)} copy(f32[10,16,8,2]{1,2,3,0:T(8,128)} %collective-permute-done.1) | data formatting | bytes 20480 | tf_op jit(solution)/shard_map/ppermute | solution.py:22
  32.1 2.4 %fusion.1 = f32[10,16,8,132]{3,0,2,1:T(8,128)S(1)} fusion(f32[1,16,8,128]{3,0,2,1:T(1,128)S(1)} %bitcast.41, f32[10,16,8,2]{3,0,2,1:T(8,128)} %copy.41, f32[9,16,8,128]{3,0,2,1:T(8,128)S(1)} %copy.55, f32[10,16,8,2]{3,0,2,1:T(8,128)S(1)} %copy.40), kind=kLoop, calls=%fused_computation.5 | loop fusion | flops 506880 | bytes 1351680 | tf_op jit(solution)/shard_map/concatenate | solution.py:23
  35.4 2.8 %fusion.10 = f32[9,16,8,129]{3,0,2,1:T(8,128)S(1)} fusion(f32[9,16,8,132]{3,0,2,1:T(8,128)S(1)} %get-tuple-element.14, f32[9,16,8,132]{3,0,2,1:T(8,128)S(1)} %get-tuple-element.13), kind=kLoop, calls=%fused_computation.21 | loop fusion | flops 1634688 | bytes 4161024 | tf_op jit(solution)/shard_map/add | solution.py:30
  38.2 2.4 %fusion.40 = f32[9,16,8,128]{3,0,2,1:T(8,128)S(1)} fusion(f32[9,16,8,128]{3,0,2,1:T(8,128)S(1)} %copy-done.2, f32[9,16,1,128]{3,0,2,1:T(8,128)} %collective-permute-done.3, f32[9,16,1,128]{3,0,2,1:T(8,128)} %collective-permute-done.2, f32[9,16,8,129]{3,0,2,1:T(8,128)S(1)} %fusion.10, f32[9,15,8,128]{3,0,2,1:T(8,128)S(1)} %slice-done, ...), kind=kOutput, calls=%fused_computation.74 | convolution fusion | flops 18137088 | bytes 5988352 | tf_op jit(solution)/shard_map/st,txyz->sxyz/dot_general | solution.py:38
  40.7 1.5 %slice_maximum_fusion = (f32[10,16,8,2]{3,0,2,1:T(8,128)}, f32[10,16,8,2]{3,0,2,1:T(8,128)S(1)}) fusion(f32[9,16,8,128]{3,0,2,1:T(8,128)S(1)} %fusion.40, f32[1,16,8,128]{3,0,2,1:T(1,128)S(1)} %bitcast.42), kind=kLoop, calls=%fused_computation.67 | loop fusion | flops 5120 | bytes 675840 | tf_op jit(solution)/shard_map/concatenate | solution.py:64
  42.2 2.4 %copy.51 = f32[10,16,8,2]{1,2,3,0:T(8,128)} copy(f32[10,16,8,2]{3,0,2,1:T(8,128)} %get-tuple-element.21) | data formatting | bytes 20480 | tf_op jit(solution)/shard_map/slice | solution.py:19
  44.6 1.3 %copy.52 = f32[10,16,8,2]{1,2,3,0:T(8,128)} copy(f32[10,16,8,2]{3,0,2,1:T(8,128)S(1)} %get-tuple-element.22) | data formatting | bytes 20480 | tf_op jit(solution)/shard_map/slice | solution.py:20
  45.9 4.7 %collective-permute-start.5 = (f32[10,16,8,2]{1,2,3,0:T(8,128)}, f32[10,16,8,2]{1,2,3,0:T(8,128)}, u32[]{:S(2)}, u32[]{:S(2)}) collective-permute-start(f32[10,16,8,2]{1,2,3,0:T(8,128)} %copy.52), channel_id=1, source_target_pairs={{4,0},{8,4},{12,8},{16,12},{20,16},{24,20},{28,24},{0,28},{5,1},{9... | collective-permute-start | bytes 30728 | tf_op jit(solution)/shard_map/ppermute | solution.py:22
  53.9 1.9 %copy.53 = f32[10,16,8,2]{3,0,2,1:T(8,128)S(1)} copy(f32[10,16,8,2]{1,2,3,0:T(8,128)} %collective-permute-done.4) | data formatting | bytes 20480 | tf_op jit(solution)/shard_map/ppermute | solution.py:21
  55.9 3.7 %collective-permute-start.7 = (f32[9,16,1,128]{3,0,2,1:T(8,128)}, f32[9,16,1,128]{3,0,2,1:T(8,128)}, u32[]{:S(2)}, u32[]{:S(2)}) collective-permute-start(f32[9,16,1,128]{3,0,2,1:T(8,128)} %get-tuple-element.26), channel_id=1, source_target_pairs={{0,1},{1,2},{2,3},{4,5},{5,6},{6,7},{8,9},{9,10},{10,11},{12,13},{... | collective-permute-start | bytes 221192 | tf_op jit(solution)/shard_map/ppermute | solution.py:21
  59.6 2.8 %copy.54 = f32[10,16,8,2]{3,0,2,1:T(8,128)} copy(f32[10,16,8,2]{1,2,3,0:T(8,128)} %collective-permute-done.5) | data formatting | bytes 20480 | tf_op jit(solution)/shard_map/ppermute | solution.py:22
  62.4 2.4 %fusion.3 = f32[10,16,8,132]{3,0,2,1:T(8,128)S(1)} fusion(f32[1,16,8,128]{3,0,2,1:T(1,128)S(1)} %bitcast.43, f32[10,16,8,2]{3,0,2,1:T(8,128)} %copy.54, f32[9,16,8,128]{3,0,2,1:T(8,128)S(1)} %fusion.40, f32[10,16,8,2]{3,0,2,1:T(8,128)S(1)} %copy.53), kind=kLoop, calls=%fused_computation.7 | loop fusion | flops 506880 | bytes 1351680 | tf_op jit(solution)/shard_map/concatenate | solution.py:23
  65.7 2.8 %fusion.5 = f32[9,16,8,129]{3,0,2,1:T(8,128)S(1)} fusion(f32[9,16,8,132]{3,0,2,1:T(8,128)S(1)} %get-tuple-element.10, f32[9,16,8,132]{3,0,2,1:T(8,128)S(1)} %get-tuple-element.9), kind=kLoop, calls=%fused_computation.10 | loop fusion | flops 1634688 | bytes 4161024 | tf_op jit(solution)/shard_map/add | solution.py:30
  68.4 4.2 %collective-permute-start.13 = (f32[9,16,1,256]{3,1,2,0:T(8,128)}, f32[9,16,1,256]{3,1,2,0:T(8,128)}, u32[]{:S(2)}, u32[]{:S(2)}) collective-permute-start(f32[9,16,1,256]{3,1,2,0:T(8,128)} %copy.76), channel_id=1, source_target_pairs={{0,1},{1,2},{2,3},{4,5},{5,6},{6,7},{8,9},{9,10},{10,11},{12,13},{... | collective-permute-start | bytes 442376 | tf_op jit(solution)/shard_map/ppermute | solution.py:21
  72.6 2.7 %fusion.32 = f32[9,16,8,128]{3,0,2,1:T(8,128)S(1)} fusion(f32[9,16,8,128]{3,0,2,1:T(8,128)S(1)} %copy-done.6, f32[9,16,1,128]{3,0,2,1:T(8,128)} %collective-permute-done.7, f32[9,16,1,128]{3,0,2,1:T(8,128)} %collective-permute-done.6, f32[9,16,8,129]{3,0,2,1:T(8,128)S(1)} %fusion.5, f32[9,15,8,128]{3,0,2,1:T(8,128)S(1)} %slice-done.2, ...), kind=kOutput, calls=%fused_computation.62 | convolution fusion | flops 18432000 | bytes 6578176 | tf_op jit(solution)/shard_map/st,txyz->sxyz/dot_general | solution.py:38
  75.5 4.7 %collective-permute-start.9 = (f32[9,8,64]{2,0,1:T(8,128)S(1)}, f32[9,8,64]{2,0,1:T(8,128)S(1)}, u32[]{:S(2)}, u32[]{:S(2)}) collective-permute-start(f32[9,8,64]{2,0,1:T(8,128)S(1)} %get-tuple-element.30), channel_id=1, source_target_pairs={{4,0},{8,4},{12,8},{16,12},{20,16},{24,20},{28,24},{0,28},{5,1},{9... | collective-permute-start | bytes 55304 | tf_op jit(solution)/shard_map/ppermute | solution.py:22
  80.2 1.3 %copy.60 = f32[9,16,8,1]{3,2,1,0:T(8,128)} copy(f32[9,16,8,1]{1,2,3,0:T(8,128)S(1)} %collective-permute-done.10) | data formatting | bytes 9216 | tf_op jit(solution)/shard_map/ppermute | solution.py:22
  81.6 2.1 %copy.62 = f32[9,16,8,1]{3,2,1,0:T(8,128)} copy(f32[9,16,8,1]{1,2,3,0:T(8,128)} %collective-permute-done.11) | data formatting | bytes 9216 | tf_op jit(solution)/shard_map/ppermute | solution.py:21
  85.7 1.7 %copy.66 = f32[9,16,1,256]{3,2,1,0:T(1,128)} copy(f32[9,16,1,256]{3,1,2,0:T(8,128)} %collective-permute-done.13) | data formatting | bytes 294912 | tf_op jit(solution)/shard_map/ppermute | solution.py:21
  88.0 2.0 %gather_fusion = f32[256,9,8]{1,2,0:T(8,128)} fusion(f32[9,8,256]{0,1,2:T(8,128)S(1)} %copy.56, s32[1024]{0:T(1024)S(1)} %get-tuple-element.38), kind=kCustom, calls=%fused_computation.clone | custom fusion | bytes 148480 | tf_op jit(solution)/shard_map/jit(_take)/gather | solution.py:79
  90.1 2.0 %gather_fusion.1 = f32[256,9,8]{1,2,0:T(8,128)} fusion(f32[9,8,256]{0,1,2:T(8,128)S(1)} %copy.56, s32[1024]{0:T(1024)S(1)} %get-tuple-element.37), kind=kCustom, calls=%fused_computation.1.clone | custom fusion | bytes 148480 | tf_op jit(solution)/shard_map/jit(_take)/gather | solution.py:80
  92.1 3.7 %fusion.44 = f32[9,1,8,256]{0,2,3,1:T(8,128)S(1)} fusion(f32[256,9,8]{1,2,0:T(8,128)} %gather_fusion.1, f32[256,9,8]{1,2,0:T(8,128)} %gather_fusion, f32[256]{0:T(256)S(1)} %bitcast.47, f32[256]{0:T(256)S(1)} %broadcast_subtract_fusion, pred[256]{0:T(512)(128)(4,1)S(1)} %copy-done.11, pred[256]{0:T(512)(128)(4,1)S(1)} %get-tuple-element.31), kind=kLoop, calls=%fused_computation.83 | loop fusion | flops 92160 | bytes 223744 | tf_op jit(solution)/shard_map/broadcast_in_dim | solution.py:50
  96.8 3.4 %fusion.18 = f32[9,16,8,256]{3,2,1,0:T(8,128)} fusion(f32[9,16,8,256]{3,2,1,0:T(8,128)S(1)} %copy-done.4, f32[9,16,1,256]{3,2,1,0:T(1,128)} %copy.66, f32[9,16,1,256]{3,2,1,0:T(1,128)S(1)} %copy.64, f32[9,16,8,1]{3,2,1,0:T(8,128)} %copy.62, f32[9,16,8,1]{3,2,1,0:T(8,128)} %copy.60, f32[9,15,8,256]{3,2,1,0:T(8,128)S(1)} %slice-done.1, f32[9,1,8,256]{3,2,1,0:T(8,128)} %copy.58), kind=kLoop, calls=%fused_computation.43 | loop fusion | flops 5013504 | bytes 3843072 | tf_op jit(solution)/shard_map/add | solution.py:54
  (80 shorter events, 16.0 us)
Async XLA Ops:
  0.6 37.6 %copy-start = (f32[9,9]{1,0:T(8,128)S(1)}, f32[9,9]{1,0:T(8,128)}, u32[]{:S(2)}) copy-start(f32[9,9]{1,0:T(8,128)} %param.12) | copy-start | bytes 976
  2.1 30.1 %copy-start.1 = (f32[9,16,8,128]{3,0,2,1:T(8,128)}, f32[9,16,8,128]{3,0,2,1:T(8,128)S(1)}, u32[]{:S(2)}) copy-start(f32[9,16,8,128]{3,0,2,1:T(8,128)S(1)} %copy.55) | copy-start | bytes 1769476
  4.6 15.5 %copy-start.3 = (f32[9,16,8,256]{3,2,1,0:T(8,128)S(1)}, f32[9,16,8,256]{3,2,1,0:T(8,128)}, u32[]{:S(2)}) copy-start(f32[9,16,8,256]{3,2,1,0:T(8,128)} %param.13) | copy-start | bytes 3538948
  7.1 19.0 %collective-permute-start = (f32[10,16,8,2]{1,2,3,0:T(8,128)}, f32[10,16,8,2]{1,2,3,0:T(8,128)}, u32[]{:S(2)}, u32[]{:S(2)}) collective-permute-start(f32[10,16,8,2]{1,2,3,0:T(8,128)} %copy.38), channel_id=1, source_target_pairs={{0,4},{4,8},{8,12},{12,16},{16,20},{20,24},{24,28},{28,0},{1,5},{5... | collective-permute-start | bytes 30728 | tf_op jit(solution)/shard_map/ppermute | solution.py:21
  10.1 13.4 %copy-start.10 = (s32[1,256]{1,0:T(1,128)S(1)}, s32[1,256]{1,0:T(1,128)}, u32[]{:S(2)}) copy-start(s32[1,256]{1,0:T(1,128)} %param.14) | copy-start | bytes 3076
  11.4 12.9 %copy-start.9 = (f32[1,256]{1,0:T(1,128)S(1)}, f32[1,256]{1,0:T(1,128)}, u32[]{:S(2)}) copy-start(f32[1,256]{1,0:T(1,128)} %param.15) | copy-start | bytes 3076
  11.4 16.6 %collective-permute-start.1 = (f32[10,16,8,2]{1,2,3,0:T(8,128)}, f32[10,16,8,2]{1,2,3,0:T(8,128)}, u32[]{:S(2)}, u32[]{:S(2)}) collective-permute-start(f32[10,16,8,2]{1,2,3,0:T(8,128)} %copy.39), channel_id=1, source_target_pairs={{4,0},{8,4},{12,8},{16,12},{20,16},{24,20},{28,24},{0,28},{5,1},{9... | collective-permute-start | bytes 30728 | tf_op jit(solution)/shard_map/ppermute | solution.py:22
  15.2 23.0 %collective-permute-start.2 = (f32[9,16,1,128]{3,0,2,1:T(8,128)}, f32[9,16,1,128]{3,0,2,1:T(8,128)}, u32[]{:S(2)}, u32[]{:S(2)}) collective-permute-start(f32[9,16,1,128]{3,0,2,1:T(8,128)} %get-tuple-element.27), channel_id=1, source_target_pairs={{1,0},{2,1},{3,2},{5,4},{6,5},{7,6},{9,8},{10,9},{11,10},{13,12},{... | collective-permute-start | bytes 221192 | tf_op jit(solution)/shard_map/ppermute | solution.py:22
  16.5 21.7 %collective-permute-start.3 = (f32[9,16,1,128]{3,0,2,1:T(8,128)}, f32[9,16,1,128]{3,0,2,1:T(8,128)}, u32[]{:S(2)}, u32[]{:S(2)}) collective-permute-start(f32[9,16,1,128]{3,0,2,1:T(8,128)} %get-tuple-element.28), channel_id=1, source_target_pairs={{0,1},{1,2},{2,3},{4,5},{5,6},{6,7},{8,9},{9,10},{10,11},{12,13},{... | collective-permute-start | bytes 221192 | tf_op jit(solution)/shard_map/ppermute | solution.py:21
  21.5 54.0 %collective-permute-start.10 = (f32[9,16,8,1]{1,2,3,0:T(8,128)}, f32[9,16,8,1]{1,2,3,0:T(8,128)S(1)}, u32[]{:S(2)}, u32[]{:S(2)}) collective-permute-start(f32[9,16,8,1]{1,2,3,0:T(8,128)} %copy.73), channel_id=1, source_target_pairs={{4,0},{8,4},{12,8},{16,12},{20,16},{24,20},{28,24},{0,28},{5,1},{9... | collective-permute-start | bytes 13832 | tf_op jit(solution)/shard_map/ppermute | solution.py:22
  24.3 7.8 %copy-start.7 = (f32[16,8,128]{2,1,0:T(8,128)S(1)}, f32[16,8,128]{2,1,0:T(8,128)}, u32[]{:S(2)}) copy-start(f32[16,8,128]{2,1,0:T(8,128)} %param.10) | copy-start | bytes 196612
  26.1 55.4 %collective-permute-start.11 = (f32[9,16,8,1]{1,2,3,0:T(8,128)}, f32[9,16,8,1]{1,2,3,0:T(8,128)}, u32[]{:S(2)}, u32[]{:S(2)}) collective-permute-start(f32[9,16,8,1]{1,2,3,0:T(8,128)} %copy.74), channel_id=1, source_target_pairs={{0,4},{4,8},{8,12},{12,16},{16,20},{20,24},{24,28},{28,0},{1,5},{5... | collective-permute-start | bytes 13832 | tf_op jit(solution)/shard_map/ppermute | solution.py:21
  28.1 56.6 %collective-permute-start.12 = (f32[9,16,1,256]{3,1,2,0:T(8,128)S(1)}, f32[9,16,1,256]{3,1,2,0:T(8,128)}, u32[]{:S(2)}, u32[]{:S(2)}) collective-permute-start(f32[9,16,1,256]{3,1,2,0:T(8,128)S(1)} %copy.75), channel_id=1, source_target_pairs={{1,0},{2,1},{3,2},{5,4},{6,5},{7,6},{9,8},{10,9},{11,10},{13,12},{... | collective-permute-start | bytes 442376 | tf_op jit(solution)/shard_map/ppermute | solution.py:22
  35.4 2.8 %copy-start.2 = (f32[9,16,8,128]{3,0,2,1:T(8,128)S(1)}, f32[9,16,8,128]{3,0,2,1:T(8,128)}, u32[]{:S(2)}) copy-start(f32[9,16,8,128]{3,0,2,1:T(8,128)} %copy-done.1) | copy-start | bytes 1769476
  35.4 2.8 %slice-start = ((f32[9,16,8,128]{3,0,2,1:T(8,128)}), f32[9,15,8,128]{3,0,2,1:T(8,128)S(1)}, s32[]{:S(2)}) async-start(f32[9,16,8,128]{3,0,2,1:T(8,128)} %copy-done.1), calls=%async_computation | async-start | bytes 1966080 | tf_op jit(solution)/shard_map/slice | solution.py:35
  35.4 2.8 %copy-start.12 = (f32[16,8,128]{2,1,0:T(8,128)S(1)}, f32[16,8,128]{2,1,0:T(8,128)}, u32[]{:S(2)}) copy-start(f32[16,8,128]{2,1,0:T(8,128)} %param.11) | copy-start | bytes 196612
  40.7 21.7 %copy-start.5 = (f32[9,16,8,128]{3,0,2,1:T(8,128)}, f32[9,16,8,128]{3,0,2,1:T(8,128)S(1)}, u32[]{:S(2)}) copy-start(f32[9,16,8,128]{3,0,2,1:T(8,128)S(1)} %fusion.40) | copy-start | bytes 1769476
  44.6 8.1 %collective-permute-start.4 = (f32[10,16,8,2]{1,2,3,0:T(8,128)}, f32[10,16,8,2]{1,2,3,0:T(8,128)}, u32[]{:S(2)}, u32[]{:S(2)}) collective-permute-start(f32[10,16,8,2]{1,2,3,0:T(8,128)} %copy.51), channel_id=1, source_target_pairs={{0,4},{4,8},{8,12},{12,16},{16,20},{20,24},{24,28},{28,0},{1,5},{5... | collective-permute-start | bytes 30728 | tf_op jit(solution)/shard_map/ppermute | solution.py:21
  45.9 9.9 %collective-permute-start.5 = (f32[10,16,8,2]{1,2,3,0:T(8,128)}, f32[10,16,8,2]{1,2,3,0:T(8,128)}, u32[]{:S(2)}, u32[]{:S(2)}) collective-permute-start(f32[10,16,8,2]{1,2,3,0:T(8,128)} %copy.52), channel_id=1, source_target_pairs={{4,0},{8,4},{12,8},{16,12},{20,16},{24,20},{28,24},{0,28},{5,1},{9... | collective-permute-start | bytes 30728 | tf_op jit(solution)/shard_map/ppermute | solution.py:22
  52.7 15.8 %collective-permute-start.6 = (f32[9,16,1,128]{3,0,2,1:T(8,128)}, f32[9,16,1,128]{3,0,2,1:T(8,128)}, u32[]{:S(2)}, u32[]{:S(2)}) collective-permute-start(f32[9,16,1,128]{3,0,2,1:T(8,128)} %get-tuple-element.25), channel_id=1, source_target_pairs={{1,0},{2,1},{3,2},{5,4},{6,5},{7,6},{9,8},{10,9},{11,10},{13,12},{... | collective-permute-start | bytes 221192 | tf_op jit(solution)/shard_map/ppermute | solution.py:22
  55.9 16.7 %collective-permute-start.7 = (f32[9,16,1,128]{3,0,2,1:T(8,128)}, f32[9,16,1,128]{3,0,2,1:T(8,128)}, u32[]{:S(2)}, u32[]{:S(2)}) collective-permute-start(f32[9,16,1,128]{3,0,2,1:T(8,128)} %get-tuple-element.26), channel_id=1, source_target_pairs={{0,1},{1,2},{2,3},{4,5},{5,6},{6,7},{8,9},{9,10},{10,11},{12,13},{... | collective-permute-start | bytes 221192 | tf_op jit(solution)/shard_map/ppermute | solution.py:21
  65.6 7.0 %copy-start.6 = (f32[9,16,8,128]{3,0,2,1:T(8,128)S(1)}, f32[9,16,8,128]{3,0,2,1:T(8,128)}, u32[]{:S(2)}) copy-start(f32[9,16,8,128]{3,0,2,1:T(8,128)} %copy-done.5) | copy-start | bytes 1769476
  65.6 7.0 %slice-start.2 = ((f32[9,16,8,128]{3,0,2,1:T(8,128)}), f32[9,15,8,128]{3,0,2,1:T(8,128)S(1)}, s32[]{:S(2)}) async-start(f32[9,16,8,128]{3,0,2,1:T(8,128)} %copy-done.5), calls=%async_computation.2 | async-start | bytes 1966080 | tf_op jit(solution)/shard_map/slice | solution.py:35
  65.6 7.0 %copy-start.8 = (f32[9,16,8,128]{3,2,1,0:T(8,128)S(1)}, f32[9,16,8,128]{3,2,1,0:T(8,128)}, u32[]{:S(2)}) copy-start(f32[9,16,8,128]{3,2,1,0:T(8,128)} %param.9) | copy-start | bytes 1769476
  65.6 7.0 %copy-start.13 = (f32[16,8,128]{2,1,0:T(8,128)S(1)}, f32[16,8,128]{2,1,0:T(8,128)}, u32[]{:S(2)}) copy-start(f32[16,8,128]{2,1,0:T(8,128)} %param.11) | copy-start | bytes 196612
  68.4 17.3 %collective-permute-start.13 = (f32[9,16,1,256]{3,1,2,0:T(8,128)}, f32[9,16,1,256]{3,1,2,0:T(8,128)}, u32[]{:S(2)}, u32[]{:S(2)}) collective-permute-start(f32[9,16,1,256]{3,1,2,0:T(8,128)} %copy.76), channel_id=1, source_target_pairs={{0,1},{1,2},{2,3},{4,5},{5,6},{6,7},{8,9},{9,10},{10,11},{12,13},{... | collective-permute-start | bytes 442376 | tf_op jit(solution)/shard_map/ppermute | solution.py:21
  75.5 12.0 %collective-permute-start.8 = (f32[9,8,64]{2,0,1:T(8,128)S(1)}, f32[9,8,64]{2,0,1:T(8,128)S(1)}, u32[]{:S(2)}, u32[]{:S(2)}) collective-permute-start(f32[9,8,64]{2,0,1:T(8,128)S(1)} %get-tuple-element.29), channel_id=1, source_target_pairs={{0,4},{4,8},{8,12},{12,16},{16,20},{20,24},{24,28},{28,0},{1,5},{5... | collective-permute-start | bytes 55304 | tf_op jit(solution)/shard_map/ppermute | solution.py:21
  75.5 11.9 %collective-permute-start.9 = (f32[9,8,64]{2,0,1:T(8,128)S(1)}, f32[9,8,64]{2,0,1:T(8,128)S(1)}, u32[]{:S(2)}, u32[]{:S(2)}) collective-permute-start(f32[9,8,64]{2,0,1:T(8,128)S(1)} %get-tuple-element.30), channel_id=1, source_target_pairs={{4,0},{8,4},{12,8},{16,12},{20,16},{24,20},{28,24},{0,28},{5,1},{9... | collective-permute-start | bytes 55304 | tf_op jit(solution)/shard_map/ppermute | solution.py:22
  83.6 8.4 %copy-start.11 = (pred[256]{0:T(512)(128)(4,1)S(1)}, pred[256]{0:T(512)(128)(4,1)}, u32[]{:S(2)}) copy-start(pred[256]{0:T(512)(128)(4,1)} %get-tuple-element.32) | copy-start | bytes 772
  92.1 4.7 %copy-start.4 = (f32[9,16,8,256]{3,2,1,0:T(8,128)S(1)}, f32[9,16,8,256]{3,2,1,0:T(8,128)}, u32[]{:S(2)}) copy-start(f32[9,16,8,256]{3,2,1,0:T(8,128)} %param.13) | copy-start | bytes 3538948
  92.1 4.7 %slice-start.1 = ((f32[9,16,8,256]{3,2,1,0:T(8,128)}), f32[9,15,8,256]{3,2,1,0:T(8,128)S(1)}, s32[]{:S(2)}) async-start(f32[9,16,8,256]{3,2,1,0:T(8,128)} %param.13), calls=%async_computation.1 | async-start | bytes 2211840 | tf_op jit(solution)/shard_map/slice | solution.py:50
where the time goes:
time: 101 us; the launch traced here: 100 us
  local copies, waits for them, and re-layouts  36 us (36%)
  starting transfers between devices  32.9 us (33%)
  other arithmetic  23.7 us (23%)
  matrix products  5.15 us (5%)
  waiting for transfers between devices  1.34 us (1%)
  between operations  1.05 us (1%)
    ppermute x7, starting transfers between devices, extended_2(): after = lax.ppermute(first, axis, down)  18.3 us
    ppermute x7, starting transfers between devices, extended_2(): before = lax.ppermute(last, axis, up)  14.6 us
    ppermute x4, local copies, waits for them, and re-layouts, extended_2(): after = lax.ppermute(first, axis, down)  7.95 us
    ppermute x4, local copies, waits for them, and re-layouts, extended_2(): before = lax.ppermute(last, axis, up)  7.61 us
    add x2, other arithmetic, tendency(): (-fplus[..., 0:-3] + 5.0 * fplus[..., 1:-2] + 2.0 * fplus[..., 2:-1]) / 6.0  5.53 us
    unnamed x37, local copies, waits for them, and re-layouts  5.46 us
    dot_general x2, matrix products, tendency(): jnp.einsum('st,txyz->sxyz', kinetics, centre, precision=lax.Precision.HIG...  5.15 us
    slice x3, local copies, waits for them, and re-layouts, extended_2(): last = lax.slice_in_dim(array, length - width, length, axis=dim)  5 us
  transfers between devices with their start and end apart: 14, of which 1 were waited for; matrix products, arithmetic and copies ran while one was open for 46% of the time, Pallas kernels for 0%

commit v1 on v0

v1 whole, which is shorter than its diff:
```python
import functools

import jax
import jax.numpy as jnp
from jax import lax
from jax.experimental import pallas as pl
from jax.experimental.pallas import tpu as pltpu
from jax.sharding import PartitionSpec as P

comb_step = 0.4
axial_speed = 0.5
radial_mix = 0.25
stator_speed = 0.5
pitch_mix = 0.2
stator_mix = 0.2

F32 = jnp.float32
BF16 = jnp.bfloat16
HI = lax.Precision.HIGHEST


def rows(tile):
    start = tile * 8
    return pl.ds(start if isinstance(start, int) else pl.multiple_of(start, 8), 8)


def split(value):
    high = value.astype(BF16)
    low = (value - high.astype(F32)).astype(BF16)
    return high, low


def kernel(
    n_az, n_rad, S, AX,
    q_hbm, u_hbm, rate_hbm, kin_hbm, st_hbm, idx_hbm, w_hbm,
    comb_out, st_out,
    q, u, rate, kin_in, sa, sb, idx, wgt,
    s1, source, coef, mat, whi, wlo, exit_x,
    edge1, edge2, exit_send, az1, az2, az3,
    row1, row2, rad1, rad2, srow, srad,
    load_sem, az_send, az_recv, rad_send, rad_recv,
):
    az = lax.axis_index("az")
    rad = lax.axis_index("rad")
    left, right = lax.rem(az + n_az - 1, n_az), lax.rem(az + 1, n_az)
    has_low, has_high = rad > 0, rad < n_rad - 1

    loads = [
        pltpu.make_async_copy(q_hbm, q, load_sem.at[0]),
        pltpu.make_async_copy(u_hbm, u, load_sem.at[1]),
        pltpu.make_async_copy(st_hbm.at[:, pl.ds(0, 128)], sa, load_sem.at[2]),
        pltpu.make_async_copy(st_hbm.at[:, pl.ds(128, 128)], sb, load_sem.at[3]),
        pltpu.make_async_copy(rate_hbm, rate, load_sem.at[4]),
        pltpu.make_async_copy(kin_hbm, kin_in, load_sem.at[5]),
        pltpu.make_async_copy(idx_hbm, idx, load_sem.at[6]),
        pltpu.make_async_copy(w_hbm, wgt, load_sem.at[7]),
    ]
    for load in loads:
        load.start()

    barrier = pltpu.get_barrier_semaphore()
    for side in (left, right):
        pl.semaphore_signal(barrier, inc=1, device_id={"az": side}, device_id_type=pl.DeviceIdType.MESH)

    @pl.when(has_low)
    def _():
        pl.semaphore_signal(barrier, inc=1, device_id={"rad": rad - 1}, device_id_type=pl.DeviceIdType.MESH)

    @pl.when(has_high)
    def _():
        pl.semaphore_signal(barrier, inc=1, device_id={"rad": rad + 1}, device_id_type=pl.DeviceIdType.MESH)

    def az_copies(phase, source_ref, landing):
        out = []
        for side, target in enumerate((left, right)):
            k = phase * 2 + side
            out.append(
                pltpu.make_async_remote_copy(
                    src_ref=source_ref,
                    dst_ref=landing.at[1 - side],
                    send_sem=az_send.at[k],
                    recv_sem=az_recv.at[phase * 2 + 1 - side],
                    device_id={"az": target},
                    device_id_type=pl.DeviceIdType.MESH,
                )
            )
        return out

    def rad_copies(phase, source_ref, landing):
        out = []
        for side, target in enumerate((rad - 1, rad + 1)):
            k = phase * 2 + side
            out.append(
                pltpu.make_async_remote_copy(
                    src_ref=source_ref.at[side],
                    dst_ref=landing.at[1 - side],
                    send_sem=rad_send.at[k],
                    recv_sem=rad_recv.at[phase * 2 + 1 - side],
                    device_id={"rad": target},
                    device_id_type=pl.DeviceIdType.MESH,
                )
            )
        return out

    def rad_each(copies, act):
        @pl.when(has_low)
        def _():
            act(copies[0], 0)

        @pl.when(has_high)
        def _():
            act(copies[1], 1)

    a1 = az_copies(0, edge1.at[pl.ds(0, (S + 1) * 8), :], az1)
    a2 = az_copies(1, edge1.at[pl.ds((S + 1) * 8, S * 8), :], az2)
    a3 = az_copies(2, exit_send, az3)
    r1 = rad_copies(0, row1, rad1)
    r2 = rad_copies(1, row2, rad2)
    r3 = rad_copies(2, srow, srad)

    def rad_wait(phase, landing):
        @pl.when(has_low)
        def _():
            pltpu.make_async_copy(landing.at[0], landing.at[0], rad_recv.at[phase * 2]).wait()

        @pl.when(has_high)
        def _():
            pltpu.make_async_copy(landing.at[1], landing.at[1], rad_recv.at[phase * 2 + 1]).wait()

    lane = lax.broadcasted_iota(jnp.int32, (8, 128), 1)
    sub = lax.broadcasted_iota(jnp.int32, (8, 128), 0)

    loads[5].wait()
    size = S * 8
    spread_c = (lax.broadcasted_iota(jnp.int32, (S, size), 1) >> 3) == lax.broadcasted_iota(jnp.int32, (S, size), 0)
    spread_r = (lax.broadcasted_iota(jnp.int32, (size, S), 0) >> 3) == lax.broadcasted_iota(jnp.int32, (size, S), 1)
    same = (lax.broadcasted_iota(jnp.int32, (size, size), 0) & 7) == (lax.broadcasted_iota(jnp.int32, (size, size), 1) & 7)
    wide = jnp.dot(kin_in[...], spread_c.astype(F32), precision=HI, preferred_element_type=F32)
    full = jnp.dot(spread_r.astype(F32), wide, precision=HI, preferred_element_type=F32)
    full = jnp.where(same, full, 0.0)
    full_hi = full.astype(BF16).astype(F32)
    mat[...] = jnp.concatenate([full_hi, full_hi, full - full_hi], axis=1).astype(BF16)

    @pl.when(jnp.logical_not(has_low))
    def _():
        for landing in (rad1, rad2, srad):
            landing[0] = jnp.zeros(landing.shape[1:], F32)

    @pl.when(jnp.logical_not(has_high))
    def _():
        for landing in (rad1, rad2, srad):
            landing[1] = jnp.zeros(landing.shape[1:], F32)

    def gather_rows(field, packed, first):
        for s in range(S):
            for side, r in ((0, 0), (1, 7)):
                packed[side, pl.ds(first + s * AX, AX), :] = field[pl.ds(s * AX * 8 + r, AX, stride=8), :]

    loads[0].wait()
    gather_rows(q, row1, 0)
    for k in (1, 2, 3):
        loads[k].wait()

    def pack_first(x, edges):
        base = x * 8
        in_q = (lane >= base) & (lane < base + 4)
        in_s = (lane >= base + 4) & (lane < base + 8)
        out = []
        for s in range(S):
            tile = s * AX + x
            a = pltpu.roll(q[rows(tile), :], base + 2, 1)
            b = pltpu.roll(jnp.where(lane == 0, sa[rows(tile), :], sb[rows(tile), :]), lax.rem(base + 5, 128), 1)
            out.append(jnp.where(in_q, a, jnp.where(in_s, b, edges[s])))
        a = pltpu.roll(u[rows(x), :], base + 2, 1)
        out.append(jnp.where(in_q, a, edges[S]))
        return tuple(out)

    zero = jnp.zeros((8, 128), F32)
    edges = lax.fori_loop(0, AX, pack_first, (zero,) * (S + 1))
    for s in range(S + 1):
        edge1[pl.ds(s * 8, 8), :] = edges[s]

    n_wait = 2 + has_low.astype(jnp.int32) + has_high.astype(jnp.int32)
    pl.semaphore_wait(barrier, n_wait)
    rad_each(r1, lambda c, side: c.start())
    for c in a1:
        c.start()
    gather_rows(sa, srow, 0)
    gather_rows(sb, srow, S * AX)
    rad_each(r3, lambda c, side: c.start())

    loads[6].wait()
    loads[7].wait()
    place = (lax.broadcasted_iota(jnp.int32, (256, 256), 0) + 64) & 255
    first = idx[...]
    w = wgt[...]
    weights = jnp.where(place == first, 1.0 - w, 0.0) + jnp.where(place == first + 1, w, 0.0)
    weights_hi, weights_lo = split(weights)
    whi[...] = weights_hi
    wlo[...] = weights_lo

    def react(field):
        def step(x, carry):
            tiles = [field[rows(s * AX + x), :] for s in range(S)]
            highs = [t.astype(BF16).astype(F32) for t in tiles]
            lows = [t - h for t, h in zip(tiles, highs)]
            stack = jnp.concatenate(highs + lows + highs, axis=0).astype(BF16)
            source[pl.ds(pl.multiple_of(x * size, 8), size), :] = jnp.dot(
                mat[...], stack, preferred_element_type=F32
            )
            return carry

        lax.fori_loop(0, AX, step, 0, unroll=4)

    react(q)
    loads[4].wait()
    for c in a1:
        c.wait_recv()

    from_left = ((lane & 7) < 2) | ((lane & 7) == 4)

    def merged(landing, s):
        return jnp.where(from_left, landing[0, pl.ds(s * 8, 8), :], landing[1, pl.ds(s * 8, 8), :])

    for s in range(S + 1):
        edge2[pl.ds(s * 8, 8), :] = merged(az1, s)

    def shifts(tile, halo):
        m2 = pltpu.roll(jnp.where(lane >= 126, halo, tile), 2, 1)
        m1 = pltpu.roll(jnp.where(lane == 127, halo, tile), 1, 1)
        p1 = pltpu.roll(jnp.where(lane == 0, halo, tile), 127, 1)
        p2 = pltpu.roll(jnp.where(lane < 2, halo, tile), 126, 1)
        return m2, m1, p1, p2

    def coefficients(x, carry):
        here = u[rows(x), :]
        halo = pltpu.roll(edge2[pl.ds(S * 8, 8), :], 126 - x * 8, 1)
        m2, m1, p1, p2 = shifts(here, halo)
        base = x * 6
        coef[rows(base), :] = jnp.maximum(m2, 0.0) * (-comb_step / 6.0)
        coef[rows(base + 1), :] = comb_step * jnp.maximum(m1, 0.0) + (comb_step / 3.0) * jnp.minimum(m1, 0.0)
        coef[rows(base + 2), :] = (1.0 - comb_step * (axial_speed + 2.0 * radial_mix)) - (0.5 * comb_step) * jnp.abs(here)
        coef[rows(base + 3), :] = (-comb_step / 3.0) * jnp.maximum(p1, 0.0) - comb_step * jnp.minimum(p1, 0.0)
        coef[rows(base + 4), :] = (comb_step / 6.0) * jnp.minimum(p2, 0.0)
        coef[rows(base + 5), :] = comb_step * rate[rows(x), :]
        return carry

    lax.fori_loop(0, AX, coefficients, 0)

    def advance(field, rims, walls, s, x, scale):
        tile = s * AX + x
        here = field[rows(tile), :]
        halo = pltpu.roll(rims[pl.ds(s * 8, 8), :], 126 - x * 8, 1)
        m2, m1, p1, p2 = shifts(here, halo)
        before = field[rows(s * AX + jnp.maximum(x - 1, 0)), :]
        down = jnp.where(sub == 0, walls[0, pl.ds(tile, 1), :], pltpu.roll(here, 1, 0))
        up = jnp.where(sub == 7, walls[1, pl.ds(tile, 1), :], pltpu.roll(here, 7, 0))
        base = x * 6
        total = coef[rows(base), :] * m2 + coef[rows(base + 1), :] * m1
        total += coef[rows(base + 2), :] * here
        total += coef[rows(base + 3), :] * p1 + coef[rows(base + 4), :] * p2
        total += coef[rows(base + 5), :] * source[rows(x * S + s), :]
        return total + scale * before + (comb_step * radial_mix) * (down + up)

    def upwind(x):
        return jnp.where(x > 0, comb_step * axial_speed, 0.0)

    rad_wait(0, rad1)

    def section_one(x, edges):
        scale = upwind(x)
        base = x * 8
        inside = (lane >= base) & (lane < base + 4)
        out = []
        for s in range(S):
            value = advance(q, edge2, rad1, s, x, scale)
            s1[rows(s * AX + x), :] = value
            out.append(jnp.where(inside, pltpu.roll(value, base + 2, 1), edges[s]))
        return tuple(out)

    edges = lax.fori_loop(0, AX, section_one, (zero,) * S)
    for s in range(S):
        edge1[pl.ds((S + 1 + s) * 8, 8), :] = edges[s]
    gather_rows(s1, row2, 0)
    rad_each(r2, lambda c, side: c.start())
    for c in a2:
        c.start()

    react(s1)
    rad_wait(2, srad)

    def passage(x, carry):
        scale = jnp.where(x > 0, stator_speed, 0.0)
        for s in range(S):
            tile = s * AX + x
            a = sa[rows(tile), :]
            b = sb[rows(tile), :]
            halo = pltpu.roll(edge2[pl.ds(s * 8, 8), :], lax.rem(123 - x * 8 + 128, 128), 1)
            a_left = pltpu.roll(jnp.where(lane == 127, halo, a), 1, 1)
            a_right = pltpu.roll(jnp.where(lane == 0, b, a), 127, 1)
            b_left = pltpu.roll(jnp.where(lane == 127, a, b), 1, 1)
            b_right = pltpu.roll(jnp.where(lane == 0, halo, b), 127, 1)
            old = s * AX + jnp.maximum(x - 1, 0)
            for k, (here, lft, rgt, field) in enumerate(((a, a_left, a_right, sa), (b, b_left, b_right, sb))):
                part = pl.ds(k * 128, 128)
                down = jnp.where(sub == 0, srad[0, pl.ds(k * S * AX + tile, 1), :], pltpu.roll(here, 1, 0))
                up = jnp.where(sub == 7, srad[1, pl.ds(k * S * AX + tile, 1), :], pltpu.roll(here, 7, 0))
                st_out[rows(tile), part] = (
                    (1.0 - stator_speed - 2.0 * pitch_mix - 2.0 * stator_mix) * here
                    + scale * field[rows(old), :]
                    + pitch_mix * (lft + rgt)
                    + stator_mix * (down + up)
                )
        return carry

    lax.fori_loop(0, AX, passage, 0)

    for c in a2:
        c.wait_recv()
    rad_wait(1, rad2)
    for s in range(S):
        exit_x[pl.ds(s * 8, 8), :] = merged(az2, s)

    def section_two(x):
        scale = upwind(x)
        for s in range(S):
            tile = s * AX + x
            value = 0.5 * (q[rows(tile), :] + advance(s1, exit_x, rad2, s, x, scale))
            comb_out[rows(tile), :] = value
            yield s, value

    for s, value in section_two(AX - 1):
        exit_send[pl.ds(s * 8, 8), :] = value
    for c in a3:
        c.start()

    def rest(x, carry):
        for _ in section_two(x):
            pass
        return carry

    lax.fori_loop(0, AX - 1, rest, 0)

    own = exit_send[...]
    for c in a3:
        c.wait_recv()
    wide_lane = lax.broadcasted_iota(jnp.int32, (size, 128), 1)
    rim = jnp.where(wide_lane < 64, az3[1], az3[0])
    cells = jnp.concatenate([own, rim], axis=1)
    cells_hi, cells_lo = split(cells)
    inflow = jnp.dot(cells_hi, whi[...], preferred_element_type=F32)
    inflow += jnp.dot(cells_lo, whi[...], preferred_element_type=F32)
    inflow += jnp.dot(cells_hi, wlo[...], preferred_element_type=F32)
    for s in range(S):
        st_out[rows(s * AX), :] += stator_speed * inflow[s * 8 : s * 8 + 8, :]

    for c in a1 + a2 + a3:
        c.wait_send()
    for copies in (r1, r2, r3):
        rad_each(copies, lambda c, side: c.wait_send())


def body(
    n_az, n_rad, combustor_state, swirl_speed, reaction_rate, kinetics, stator_state, inlet_index, inlet_weight
):
    S, AX, NR, CA = combustor_state.shape
    pitch = stator_state.shape[3]
    tiles = S * AX
    VM = pltpu.VMEM
    dma = pltpu.SemaphoreType.DMA
    any_spec = pl.BlockSpec(memory_space=pl.ANY)
    comb, stator = pl.pallas_call(
        functools.partial(kernel, n_az, n_rad, S, AX),
        out_shape=(
            jax.ShapeDtypeStruct((tiles * 8, 128), F32),
            jax.ShapeDtypeStruct((tiles * 8, 256), F32),
        ),
        in_specs=[any_spec] * 7,
        out_specs=(pl.BlockSpec(memory_space=VM), pl.BlockSpec(memory_space=VM)),
        scratch_shapes=[
            VM((tiles * 8, 128), F32),
            VM((AX * 8, 128), F32),
            VM((AX * 8, 128), F32),
            VM((S, S), F32),
            VM((tiles * 8, 128), F32),
            VM((tiles * 8, 128), F32),
            VM((1, 256), jnp.int32),
            VM((1, 256), F32),
            VM((tiles * 8, 128), F32),
            VM((tiles * 8, 128), F32),
            VM((AX * 6 * 8, 128), F32),
            VM((S * 8, S * 24), BF16),
            VM((256, 256), BF16),
            VM((256, 256), BF16),
            VM((S * 8, 128), F32),
            VM(((2 * S + 1) * 8, 128), F32),
            VM(((S + 1) * 8, 128), F32),
            VM((S * 8, 128), F32),
            VM((2, (S + 1) * 8, 128), F32),
            VM((2, S * 8, 128), F32),
            VM((2, S * 8, 128), F32),
            VM((2, tiles, 128), F32),
            VM((2, tiles, 128), F32),
            VM((2, tiles, 128), F32),
            VM((2, tiles, 128), F32),
            VM((2, 2 * tiles, 128), F32),
            VM((2, 2 * tiles, 128), F32),
            dma((8,)),
            dma((6,)),
            dma((6,)),
            dma((6,)),
            dma((6,)),
        ],
        compiler_params=pltpu.CompilerParams(
            collective_id=0, has_side_effects=True, vmem_limit_bytes=40 * 1024 * 1024
        ),
        cost_estimate=pl.CostEstimate(flops=40000000, bytes_accessed=4000000, transcendentals=0),
    )(
        combustor_state.reshape(tiles * NR, CA),
        swirl_speed.reshape(AX * NR, CA),
        reaction_rate.reshape(AX * NR, CA),
        kinetics,
        stator_state.reshape(tiles * NR, pitch),
        inlet_index,
        inlet_weight,
    )
    return (comb.reshape(combustor_state.shape), stator.reshape(stator_state.shape))


def solution(mesh):
    in_specs = (
        P(None, None, "rad", "az"),
        P(None, "rad", "az"),
        P(None, "rad", "az"),
        P(),
        P(None, None, "rad", "az"),
        P("az", None),
        P("az", None),
    )
    out_specs = (P(None, None, "rad", "az"), P(None, None, "rad", "az"))
    return jax.shard_map(
        functools.partial(body, mesh.shape["az"], mesh.shape["rad"]),
        mesh=mesh,
        in_specs=in_specs,
        out_specs=out_specs,
        check_vma=False,
    )
```

time: 101 us -> 34.8 us (0.34)
  starting transfers between devices: 32.9 us -> 0 us
  local copies, waits for them, and re-layouts: 36 us -> 7.89 us
  Pallas kernels: 0 us -> 25.9 us
  other arithmetic: 23.7 us -> 0 us
  matrix products: 5.15 us -> 0 us
  waiting for transfers between devices: 1.34 us -> 0 us
    ppermute x14 -> x0, starting transfers between devices: 32.9 us -> none  [the longest x7 18.3 us: extended_2(): after = lax.ppermute(first, axis, down)]
    pallas_call x0 -> x1, Pallas kernels: none -> 25.9 us  [body(): pl.pallas_call(functools.partial(kernel, n_az, n_rad, S, AX), out_shape=(...]
    ppermute x8 -> x0, local copies, waits for them, and re-layouts: 15.6 us -> none  [the longest x4 7.95 us: extended_2(): after = lax.ppermute(first, axis, down)]
    slice x15 -> x0, local copies, waits for them, and re-layouts: 9.54 us -> none  [the longest x3 5 us: extended_2(): last = lax.slice_in_dim(array, length - width, length, axis=dim)]
    add x3 -> x0, other arithmetic: 8.94 us -> none  [the longest x2 5.53 us: tendency(): (-fplus[..., 0:-3] + 5.0 * fplus[..., 1:-2] + 2.0 * fplus[..., 2:-1]) / 6.0]
    concatenate x5 -> x0, other arithmetic: 8.87 us -> none  [the longest x3 4.86 us: extended_2(): array = jnp.concatenate([before, array, after], axis=dim)]
    dot_general x2 -> x0, matrix products: 5.15 us -> none  [tendency(): jnp.einsum('st,txyz->sxyz', kinetics, centre, precision=lax.Precision.HIG...]
    gather x2 -> x0, local copies, waits for them, and re-layouts: 4.02 us -> none  [the longest x1 2.03 us: body(): left_value = jnp.take(exit_rim, offsets, axis=2)]
  transfers between devices with their start and end apart: 14 -> 0, of which waited for: 1 -> 0; matrix products, arithmetic and copies ran while one was open for 46% -> 0% of each run, Pallas kernels for 0% -> 0%
where the time goes in v1:
time: 34.8 us; the launch traced here: 34.4 us
  Pallas kernels  25.9 us (74%)
  local copies, waits for them, and re-layouts  7.89 us (23%)
  between operations  0.66 us (2%)
    pallas_call x1, Pallas kernels, body(): pl.pallas_call(functools.partial(kernel, n_az, n_rad, S, AX), out_shape=(...  25.9 us
    unnamed x16, local copies, waits for them, and re-layouts  7.89 us

profile of v1, /device:TPU:0, one launch (start us, length us, event | category | flops | bytes accessed | tf_op | source)
XLA Modules:
  0.0 34.4 jit_solution(5842245080804393654)
XLA Ops:
  0.6 0.0 copy-start
  0.6 1.3 %copy-done = f32[9,16,8,256]{3,2,1,0:T(8,128)S(1)} copy-done((f32[9,16,8,256]{3,2,1,0:T(8,128)S(1)}, f32[9,16,8,256]{3,2,1,0:T(8,128)}, u32[]{:S(2)}) %copy-start) | copy-done | bytes 1179672
  1.9 0.0 copy-start.1
  1.9 1.1 %copy-done.1 = f32[9,16,8,128]{3,2,1,0:T(8,128)S(1)} copy-done((f32[9,16,8,128]{3,2,1,0:T(8,128)S(1)}, f32[9,16,8,128]{3,2,1,0:T(8,128)}, u32[]{:S(2)}) %copy-start.1) | copy-done | bytes 589848
  3.0 0.0 copy-start.2
  3.0 0.8 %copy-done.2 = f32[16,8,128]{2,1,0:T(8,128)S(1)} copy-done((f32[16,8,128]{2,1,0:T(8,128)S(1)}, f32[16,8,128]{2,1,0:T(8,128)}, u32[]{:S(2)}) %copy-start.2) | copy-done | bytes 65560
  3.8 0.0 copy-start.3
  3.8 0.8 %copy-done.3 = f32[16,8,128]{2,1,0:T(8,128)S(1)} copy-done((f32[16,8,128]{2,1,0:T(8,128)S(1)}, f32[16,8,128]{2,1,0:T(8,128)}, u32[]{:S(2)}) %copy-start.3) | copy-done | bytes 65560
  4.6 0.0 copy-start.4
  4.7 0.7 %copy-done.4 = f32[9,9]{1,0:T(8,128)S(1)} copy-done((f32[9,9]{1,0:T(8,128)S(1)}, f32[9,9]{1,0:T(8,128)}, u32[]{:S(2)}) %copy-start.4) | copy-done | bytes 348
  5.3 0.0 copy-start.5
  5.3 0.7 %copy-done.5 = s32[1,256]{1,0:T(1,128)S(1)} copy-done((s32[1,256]{1,0:T(1,128)S(1)}, s32[1,256]{1,0:T(1,128)}, u32[]{:S(2)}) %copy-start.5) | copy-done | bytes 1048
  6.0 0.0 copy-start.6
  6.0 0.7 %copy-done.6 = f32[1,256]{1,0:T(1,128)S(1)} copy-done((f32[1,256]{1,0:T(1,128)S(1)}, f32[1,256]{1,0:T(1,128)}, u32[]{:S(2)}) %copy-start.6) | copy-done | bytes 1048
  6.7 25.9 %shard_map.86 = (f32[1152,128]{1,0:T(8,128)S(1)}, f32[1152,256]{1,0:T(8,128)S(1)}) custom-call(f32[1152,128]{1,0:T(8,128)S(1)} %bitcast.9, f32[128,128]{1,0:T(8,128)S(1)} %bitcast.10, f32[128,128]{1,0:T(8,128)S(1)} %bitcast.11, f32[9,9]{1,0:T(8,128)S(1)} %copy-done.4, f32[1152,256]{1,0:T(8,128)S(1)} %bitcast.6, s32[1,256]{1,0:T(1,128)S(1)} %copy-done.5, ...), custom_call_target="tpu_custom_call" | custom-call | flops 40000000 | bytes 4000000 | tf_op jit(solution)/shard_map/pallas_call | solution.py:372
  32.6 0.8 %copy.11 = f32[9,16,8,128]{3,2,1,0:T(8,128)} copy(f32[9,16,8,128]{3,2,1,0:T(8,128)S(1)} %bitcast.8) | data formatting | bytes 1179648
  33.4 1.0 %copy.12 = f32[9,16,8,256]{3,2,1,0:T(8,128)} copy(f32[9,16,8,256]{3,2,1,0:T(8,128)S(1)} %bitcast.7) | data formatting | bytes 2359296
Async XLA Ops:
  0.6 1.3 %copy-start = (f32[9,16,8,256]{3,2,1,0:T(8,128)S(1)}, f32[9,16,8,256]{3,2,1,0:T(8,128)}, u32[]{:S(2)}) copy-start(f32[9,16,8,256]{3,2,1,0:T(8,128)} %param.11) | copy-start | bytes 3538948
  1.9 1.1 %copy-start.1 = (f32[9,16,8,128]{3,2,1,0:T(8,128)S(1)}, f32[9,16,8,128]{3,2,1,0:T(8,128)}, u32[]{:S(2)}) copy-start(f32[9,16,8,128]{3,2,1,0:T(8,128)} %param.7) | copy-start | bytes 1769476
  3.0 0.8 %copy-start.2 = (f32[16,8,128]{2,1,0:T(8,128)S(1)}, f32[16,8,128]{2,1,0:T(8,128)}, u32[]{:S(2)}) copy-start(f32[16,8,128]{2,1,0:T(8,128)} %param.8) | copy-start | bytes 196612
  3.8 0.8 %copy-start.3 = (f32[16,8,128]{2,1,0:T(8,128)S(1)}, f32[16,8,128]{2,1,0:T(8,128)}, u32[]{:S(2)}) copy-start(f32[16,8,128]{2,1,0:T(8,128)} %param.9) | copy-start | bytes 196612
  4.6 0.7 %copy-start.4 = (f32[9,9]{1,0:T(8,128)S(1)}, f32[9,9]{1,0:T(8,128)}, u32[]{:S(2)}) copy-start(f32[9,9]{1,0:T(8,128)} %kin_hbm.1) | copy-start | bytes 976
  5.3 0.7 %copy-start.5 = (s32[1,256]{1,0:T(1,128)S(1)}, s32[1,256]{1,0:T(1,128)}, u32[]{:S(2)}) copy-start(s32[1,256]{1,0:T(1,128)} %idx_hbm.1) | copy-start | bytes 3076
  6.0 0.7 %copy-start.6 = (f32[1,256]{1,0:T(1,128)S(1)}, f32[1,256]{1,0:T(1,128)}, u32[]{:S(2)}) copy-start(f32[1,256]{1,0:T(1,128)} %w_hbm.1) | copy-start | bytes 3076

commit v2 on v1

--- a/solution.py
+++ b/solution.py
@@ -176,7 +176,7 @@
         return tuple(out)
 
     zero = jnp.zeros((8, 128), F32)
-    edges = lax.fori_loop(0, AX, pack_first, (zero,) * (S + 1))
+    edges = lax.fori_loop(0, AX, pack_first, (zero,) * (S + 1), unroll=2)
     for s in range(S + 1):
         edge1[pl.ds(s * 8, 8), :] = edges[s]
 
@@ -210,7 +210,7 @@
             )
             return carry
 
-        lax.fori_loop(0, AX, step, 0, unroll=4)
+        lax.fori_loop(0, AX, step, 0, unroll=16)
 
     react(q)
     loads[4].wait()
@@ -245,7 +245,7 @@
         coef[rows(base + 5), :] = comb_step * rate[rows(x), :]
         return carry
 
-    lax.fori_loop(0, AX, coefficients, 0)
+    lax.fori_loop(0, AX, coefficients, 0, unroll=4)
 
     def advance(field, rims, walls, s, x, scale):
         tile = s * AX + x
@@ -278,7 +278,7 @@
             out.append(jnp.where(inside, pltpu.roll(value, base + 2, 1), edges[s]))
         return tuple(out)
 
-    edges = lax.fori_loop(0, AX, section_one, (zero,) * S)
+    edges = lax.fori_loop(0, AX, section_one, (zero,) * S, unroll=2)
     for s in range(S):
         edge1[pl.ds((S + 1 + s) * 8, 8), :] = edges[s]
     gather_rows(s1, row2, 0)
@@ -313,7 +313,7 @@
                 )
         return carry
 
-    lax.fori_loop(0, AX, passage, 0)
+    lax.fori_loop(0, AX, passage, 0, unroll=2)
 
     for c in a2:
         c.wait_recv()
@@ -339,7 +339,7 @@
             pass
         return carry
 
-    lax.fori_loop(0, AX - 1, rest, 0)
+    lax.fori_loop(0, AX - 1, rest, 0, unroll=3)
 
     own = exit_send[...]
     for c in a3:
@@ -412,7 +412,7 @@
             dma((6,)),
         ],
         compiler_params=pltpu.CompilerParams(
-            collective_id=0, has_side_effects=True, vmem_limit_bytes=40 * 1024 * 1024
+            collective_id=0, has_side_effects=True, vmem_limit_bytes=58 * 1024 * 1024
         ),
         cost_estimate=pl.CostEstimate(flops=40000000, bytes_accessed=4000000, transcendentals=0),
     )(

time: 34.8 us -> 27.9 us (0.80)
  local copies, waits for them, and re-layouts: 7.89 us -> 3.03 us
  Pallas kernels: 25.9 us -> 24 us
    unnamed x16 -> x4, local copies, waits for them, and re-layouts: 7.89 us -> 3.03 us
    pallas_call x1, Pallas kernels: 25.9 us -> 24 us  [body(): pl.pallas_call(functools.partial(kernel, n_az, n_rad, S, AX), out_shape=(...]
where the time goes in v2:
time: 27.9 us; the launch traced here: 27.7 us
  Pallas kernels  24 us (86%)
  local copies, waits for them, and re-layouts  3.03 us (11%)
  between operations  0.65 us (2%)
    pallas_call x1, Pallas kernels, body(): pl.pallas_call(functools.partial(kernel, n_az, n_rad, S, AX), out_shape=(...  24 us
    unnamed x4, local copies, waits for them, and re-layouts  3.03 us

profile of v2, /device:TPU:0, one launch (start us, length us, event | category | flops | bytes accessed | tf_op | source)
XLA Modules:
  0.0 27.7 jit_solution(6007393783718134342)
XLA Ops:
  0.6 24.0 %shard_map.86 = (f32[1152,128]{1,0:T(8,128)}, f32[1152,256]{1,0:T(8,128)}) custom-call(f32[1152,128]{1,0:T(8,128)} %bitcast.9, f32[128,128]{1,0:T(8,128)} %bitcast.10, f32[128,128]{1,0:T(8,128)} %bitcast.11, f32[9,9]{1,0:T(8,128)} %kin_hbm.1, f32[1152,256]{1,0:T(8,128)} %bitcast.6, s32[1,256]{1,0:T(1,128)} %idx_hbm.1, f32[1,256]{1,0:T(1,128)} %w_hbm.1), custom_call_target="tpu_custom_call" | custom-call | flops 40000000 | bytes 4000000 | tf_op jit(solution)/shard_map/pallas_call | solution.py:372
  24.7 0.0 copy-start
  24.7 2.0 %copy.11 = f32[9,16,8,128]{3,2,1,0:T(8,128)} copy(f32[9,16,8,128]{3,2,1,0:T(8,128)} %bitcast.8) | data formatting | bytes 1179648
  26.7 0.0 copy-done
  26.7 1.0 %copy.12 = f32[9,16,8,256]{3,2,1,0:T(8,128)} copy(f32[9,16,8,256]{3,2,1,0:T(8,128)S(1)} %bitcast.7) | data formatting | bytes 2359296
Async XLA Ops:
  24.7 2.0 %copy-start = (f32[1152,256]{1,0:T(8,128)S(1)}, f32[1152,256]{1,0:T(8,128)}, u32[]{:S(2)}) copy-start(f32[1152,256]{1,0:T(8,128)} %get-tuple-element.5) | copy-start | bytes 3538948
